TPU v7x, 32 devices: a whole 2x2x4 slice. The times are simulated.
32 devices in a mesh: dom: 16 (over z, y, x), sub: 2 (over core).
Axes of the slice: x: 2, y: 2, z: 4, core: 2. Of those that a mesh axis runs over, the one named last changes fastest.
Arguments:
- coupling: bfloat16 [16, 2, 16, 8, 128, 256], P('dom', 'sub'), as said below
- null_vector: bfloat16 [16, 2, 16, 128], P('dom', 'sub'), may hold values from 0.5 to 2
- aggregate_ids: int32 [16, 2, 16, 128], P('dom', 'sub'), may hold values from 0 to 31, as said below
- send_list: int32 [16, 16, 2], P('dom'), may hold values from -1 to 15, as said below
- recv_list: int32 [16, 16, 8], P('dom'), may hold values from 0 to 47, as said below
Outputs:
- coarse_tiles: float32 [256, 32, 256], P('dom', 'sub')
Inputs may be any that keep to these rules, and one draw needn't show every extreme that they name: `aggregate_ids`: within each coarse block (both halves together) every aggregate id 0 to 31 is used by at least one fine row. The neighbours of partition d are the six partitions d + 1, d - 1, d + 2, d - 2, d + 4, d - 4 modulo 16. Each neighbour p of d fills all 2 slots of send_list[p, d]; every other entry is -1. Each filled slot is named by one or more entries of recv_list[d]. recv_list[d, b, 0] = b; for k = 1 to 3 it is another block of partition d (not b); for k = 4 to 7 it is 16 + p * 2 + c for a neighbour p of d, the four neighbours of one block row distinct. coupling[d, s, b, 0, i, s * 128 + i] lies between 2 and 4.
All inputs are finite; a program needn't handle non-finite values.
Results may differ from a plain program's by a relative error of at most 0.0061.
Values may be sent and summed in bfloat16 or wider, within the bound.
A program may use at most 64 MiB of HBM per device.

v0:
```python
import jax
import jax.numpy as jnp
from jax import lax
from jax.sharding import PartitionSpec as P

AGGS = 32


OMEGA = 0.6666667
OFFSETS = (1, -1, 2, -2, 4, -4)


def passed_along(value, axis, steps):
    count = lax.axis_size(axis)
    pairs = [(source, (source + steps) % count) for source in range(count)]
    return lax.ppermute(value, axis, pairs)


def partner_2(value, axis, stride):
    mask = 2**stride
    pairs = [(source, source ^ mask) for source in range(lax.axis_size(axis))]
    return lax.ppermute(value, axis, pairs)


def per_device(coupling, null_vector, aggregate_ids, send_list, recv_list):
    couple_tiles = coupling[0, 0]
    null_rows = null_vector[0, 0]
    aggregate = aggregate_ids[0, 0]
    send_rows = send_list[0]
    receives = recv_list[0]
    blocks, neigh, fine_rows, span_cols = couple_tiles.shape
    slot_count = send_rows.shape[1]
    domains = lax.axis_size("dom")
    groups = AGGS
    labels = jnp.arange(groups, dtype=jnp.int32)
    scattered = jnp.where(
        aggregate[:, None, :] == labels[None, :, None],
        null_rows[:, None, :],
        jnp.zeros((), jnp.bfloat16),
    )
    gathered = lax.all_gather(scattered, "sub", axis=2, tiled=True).astype(jnp.float32)
    tentative = (gathered / jnp.sqrt(jnp.sum(gathered * gathered, axis=-1, keepdims=True))).astype(
        jnp.bfloat16
    )
    sub_index = lax.axis_index("sub")
    own_rows = lax.dynamic_slice_in_dim(tentative, sub_index * fine_rows, fine_rows, 2).astype(
        jnp.float32
    )
    diag_tile = couple_tiles[:, 0]
    diag_square = lax.dynamic_slice_in_dim(diag_tile, sub_index * fine_rows, fine_rows, 2)
    diag_vals = jnp.diagonal(diag_square, axis1=1, axis2=2).astype(jnp.float32)
    smoothing = jnp.einsum("bgj,bij->bgi", tentative, diag_tile, preferred_element_type=jnp.float32)
    smoothed = (own_rows - OMEGA * smoothing / diag_vals[:, None, :]).astype(jnp.bfloat16)
    my_dom = lax.axis_index("dom")
    pieces = []
    for offset in OFFSETS:
        target = (my_dom + offset + domains) % domains
        chosen = jnp.clip(
            lax.dynamic_index_in_dim(send_rows, target, 0, keepdims=False), 0, blocks - 1
        )
        payload = smoothed[chosen]
        pieces.append(passed_along(payload, "dom", offset))
    arrived = jnp.concatenate(pieces, axis=0)
    prolong, arrived = (
        lax.all_gather(smoothed, "sub", axis=2, tiled=True),
        lax.all_gather(arrived, "sub", axis=2, tiled=True),
    )
    offset_table = (jnp.array(OFFSETS, jnp.int32) + domains) % domains
    shifted = receives - blocks
    is_remote = shifted >= 0
    safe_shift = jnp.maximum(shifted, 0)
    source = safe_shift // slot_count
    slot_index = safe_shift % slot_count
    distance = (my_dom - source + domains) % domains
    matches = (distance[..., None] == offset_table).astype(jnp.int32)
    position = jnp.sum(matches * jnp.arange(len(OFFSETS), dtype=jnp.int32), axis=-1)
    lookup = jnp.where(is_remote, blocks + position * slot_count + slot_index, receives)
    sources = jnp.concatenate([prolong, arrived], axis=0)
    partner = sources[lookup]
    left_part = jnp.einsum(
        "bgi,bkij->bkgj", smoothed, couple_tiles, preferred_element_type=jnp.float32
    ).astype(jnp.bfloat16)
    coarse = jnp.einsum("bkgj,bkhj->bgkh", left_part, partner, preferred_element_type=jnp.float32)
    coarse = coarse.reshape(blocks, groups, neigh * groups)
    summed = lax.psum_scatter(coarse, "sub", scatter_dimension=1, tiled=True)
    half_blocks = blocks // 2
    parity = my_dom % 2
    kept_half = lax.dynamic_slice_in_dim(summed, parity * half_blocks, half_blocks, 0)
    given_half = lax.dynamic_slice_in_dim(summed, (1 - parity) * half_blocks, half_blocks, 0)
    partner_half = partner_2(given_half, "dom", 0)
    first_order = jnp.concatenate([kept_half, partner_half], axis=0)
    second_order = jnp.concatenate([partner_half, kept_half], axis=0)
    return jnp.where(parity == 0, first_order, second_order)


def solution(mesh):
    in_specs = (
        P("dom", "sub", None, None, None, None),
        P("dom", "sub", None, None),
        P("dom", "sub", None, None),
        P("dom", None, None),
        P("dom", None, None),
    )
    out_specs = P("dom", "sub", None)
    return jax.shard_map(
        per_device, mesh=mesh, in_specs=in_specs, out_specs=out_specs, check_vma=False
    )
```

profile of v0, /device:TPU:0, one launch (start us, length us, event | category | flops | bytes accessed | tf_op | source)
XLA Modules:
  0.0 85.4 jit_solution(11793031231373924531)
XLA Ops:
  6.5 1.2 %fusion.36 = (s32[2]{0:T(128)S(1)}, s32[2]{0:T(128)S(1)}, s32[2]{0:T(128)S(1)}, s32[2]{0:T(128)S(1)}, s32[2]{0:T(128)S(1)}, /*index=5*/s32[2]{0:T(128)S(1)}) fusion(s32[1,16,2]{1,2,0:T(2,128)} %param.9, s32[]{:T(128)S(6)} %select_n.212, s32[]{:T(128)S(6)} %select_n.206, s32[]{:T(128)S(6)} %select_n.203, s32[]{:T(128)S(6)} %select_n.200, s32[]{:T(128)S(6)} %select_n.197, ...), kind=kLoop, calls=%fused_computation.87 | loop fusion | flops 12 | bytes 120 | tf_op jit(solution)/shard_map/jit(clip)/min | solution.py:58
  7.7 7.7 %copy.27 = bf16[1,1,16,8,128,256]{5,4,2,3,1,0:T(8,128)(2,1)} copy(bf16[1,1,16,8,128,256]{5,4,3,2,1,0:T(8,128)(2,1)} %param.6) | data formatting | bytes 16777216 | tf_op args[0]
  15.4 1.3 %slice.20 = bf16[16,1,128,256]{3,2,0,1:T(8,128)(2,1)S(1)} slice(bf16[16,8,128,256]{3,2,0,1:T(8,128)(2,1)} %bitcast.79), slice={[0:16], [0:1], [0:128], [0:256]} | slice | bytes 2097152 | tf_op jit(solution)/shard_map/slice | solution.py:49
  16.9 3.2 %copy.19 = bf16[16,128,128]{0,2,1:T(8,128)(2,1)} copy(bf16[16,128,128]{2,1,0:T(8,128)(2,1)S(1)} %dynamic-slice_bitcast_fusion) | data formatting | bytes 1048576 | tf_op jit(solution)/shard_map/dynamic_slice | solution.py:50
  20.1 2.0 %gather_fusion = bf16[128,16]{1,0:T(8,128)(2,1)S(1)} fusion(bf16[16,128,128]{0,2,1:T(8,128)(2,1)} %copy.19, s32[128]{0:T(128)S(1)} %or_bitcast_fusion), kind=kCustom, calls=%fused_computation | custom fusion | bytes 9216 | tf_op jit(solution)/shard_map/jit(diagonal)/gather | solution.py:51
  22.2 2.1 %all_gather.9 = bf16[16,32,256]{2,1,0:T(8,128)(2,1)S(1)} all-gather(bf16[16,32,128]{2,1,0:T(8,128)(2,1)S(1)} %fusion.15), channel_id=1, replica_groups=mesh['dom'=16,'sub'=2] {'sub'}, dimensions={2}, use_global_device_ids=true | all-gather | bytes 393216 | tf_op jit(solution)/shard_map/all_gather | solution.py:41
  24.6 1.7 %fusion.11 = bf16[16,32,128]{2,1,0:T(8,128)(2,1)S(1)} fusion(bf16[16,32,256]{2,1,0:T(8,128)(2,1)S(1)} %fusion.14, f32[16,128]{1,0:T(8,128)S(1)} %copy.20, s32[]{:T(128)S(6)} %select_n.195, bf16[16,8,128,256]{3,2,0,1:T(8,128)(2,1)} %bitcast.80), kind=kOutput, calls=%fused_computation.17 | convolution fusion | flops 33882112 | bytes 1581060 | tf_op jit(solution)/shard_map/bgj,bij->bgi/dot_general | solution.py:52
  26.3 0.6 gather_fusion.6
  26.9 5.0 %collective-permute-start.5 = (bf16[2,32,128]{2,1,0:T(8,128)(2,1)S(1)}, bf16[2,32,128]{2,1,0:T(8,128)(2,1)S(1)}, u32[]{:S(2)}, u32[]{:S(2)}) collective-permute-start(bf16[2,32,128]{2,1,0:T(8,128)(2,1)S(1)} %gather_fusion.6), channel_id=1, source_target_pairs={{0,24},{2,26},{4,28},{6,30},{8,0},{10,2},{12,4},{14,6},{16,8},{18,... | collective-permute-start | bytes 49160 | tf_op jit(solution)/shard_map/ppermute | solution.py:16
  33.1 4.8 %collective-permute-start.3 = (bf16[2,32,128]{2,1,0:T(8,128)(2,1)S(1)}, bf16[2,32,128]{2,1,0:T(8,128)(2,1)S(1)}, u32[]{:S(2)}, u32[]{:S(2)}) collective-permute-start(bf16[2,32,128]{2,1,0:T(8,128)(2,1)S(1)} %gather_fusion.4), channel_id=1, source_target_pairs={{0,28},{2,30},{4,0},{6,2},{8,4},{10,6},{12,8},{14,10},{16,12},{18,... | collective-permute-start | bytes 49160 | tf_op jit(solution)/shard_map/ppermute | solution.py:16
  39.1 1.5 %collective-permute-start = (bf16[2,32,128]{2,1,0:T(8,128)(2,1)S(1)}, bf16[2,32,128]{2,1,0:T(8,128)(2,1)S(1)}, u32[]{:S(2)}, u32[]{:S(2)}) collective-permute-start(bf16[2,32,128]{2,1,0:T(8,128)(2,1)S(1)} %gather_fusion.1), channel_id=1, source_target_pairs={{0,2},{2,4},{4,6},{6,8},{8,10},{10,12},{12,14},{14,16},{16,18},{18... | collective-permute-start | bytes 49160 | tf_op jit(solution)/shard_map/ppermute | solution.py:16
  41.0 2.0 %all_gather.10 = bf16[16,32,256]{2,1,0:T(8,128)(2,1)S(1)} all-gather(bf16[16,32,128]{2,1,0:T(8,128)(2,1)S(1)} %fusion.11), channel_id=1, replica_groups=mesh['dom'=16,'sub'=2] {'sub'}, dimensions={2}, use_global_device_ids=true | all-gather | bytes 393216 | tf_op jit(solution)/shard_map/all_gather | solution.py:65
  43.5 3.0 %collective-permute-done = bf16[2,32,128]{2,1,0:T(8,128)(2,1)S(1)} collective-permute-done((bf16[2,32,128]{2,1,0:T(8,128)(2,1)S(1)}, bf16[2,32,128]{2,1,0:T(8,128)(2,1)S(1)}, u32[]{:S(2)}, u32[]{:S(2)}) %collective-permute-start) | collective-permute-done | bytes 16416 | tf_op jit(solution)/shard_map/ppermute | solution.py:16
  46.5 2.0 %collective-permute-start.1 = (bf16[2,32,128]{2,1,0:T(8,128)(2,1)S(1)}, bf16[2,32,128]{2,1,0:T(8,128)(2,1)S(1)}, u32[]{:S(2)}, u32[]{:S(2)}) collective-permute-start(bf16[2,32,128]{2,1,0:T(8,128)(2,1)S(1)} %gather_fusion.2), channel_id=1, source_target_pairs={{0,30},{2,0},{4,2},{6,4},{8,6},{10,8},{12,10},{14,12},{16,14},{18,... | collective-permute-start | bytes 49160 | tf_op jit(solution)/shard_map/ppermute | solution.py:16
  48.5 1.7 %collective-permute-done.1 = bf16[2,32,128]{2,1,0:T(8,128)(2,1)S(1)} collective-permute-done((bf16[2,32,128]{2,1,0:T(8,128)(2,1)S(1)}, bf16[2,32,128]{2,1,0:T(8,128)(2,1)S(1)}, u32[]{:S(2)}, u32[]{:S(2)}) %collective-permute-start.1) | collective-permute-done | bytes 16416 | tf_op jit(solution)/shard_map/ppermute | solution.py:16
  50.3 1.9 %all_gather.11 = bf16[12,32,256]{2,1,0:T(8,128)(2,1)S(1)} all-gather(bf16[12,32,128]{2,1,0:T(8,128)(2,1)S(1)} %constant_dynamic-update-slice_fusion), channel_id=1, replica_groups=mesh['dom'=16,'sub'=2] {'sub'}, dimensions={2}, use_global_device_ids=true | all-gather | bytes 294912 | tf_op jit(solution)/shard_map/all_gather | solution.py:66
  52.3 2.0 %gather_fusion.7 = bf16[128,32,256]{2,1,0:T(8,128)(2,1)} fusion(bf16[28,32,256]{2,1,0:T(8,128)(2,1)S(1)} %pad_maximum_fusion, s32[1024]{0:T(1024)S(1)} %pad_clamp_fusion), kind=kCustom, calls=%fused_computation.7 | custom fusion | bytes 4194816 | tf_op jit(solution)/shard_map/gather | solution.py:79
  54.3 5.8 %fusion.2 = f32[16,8,32,32]{3,2,1,0:T(8,128)S(1)} fusion(bf16[16,8,32,256]{3,2,1,0:T(8,128)(2,1)} %bitcast.82, bf16[1,1,16,8,128,256]{5,4,3,2,1,0:T(8,128)(2,1)} %param.6, bf16[16,32,128]{2,1,0:T(8,128)(2,1)S(1)} %fusion.11), kind=kOutput, calls=%fused_computation.11 | convolution fusion | flops 336592896 | bytes 11141120 | tf_op jit(solution)/shard_map/bkgj,bkhj->bgkh/dot_general | solution.py:83
  60.2 1.4 %copy.23 = f32[16,32,256]{2,1,0:T(8,128)} copy(f32[16,32,256]{1,2,0:T(8,128)S(1)} %bitcast.81) | data formatting | bytes 1048576 | tf_op jit(solution)/shard_map/reshape | solution.py:84
  61.6 9.5 %reduce-scatter.2.cloned.1.call-done = f32[16,16,256]{2,1,0:T(8,128)} async-done(((f32[16,32,256]{2,1,0:T(8,128)}), f32[16,16,256]{2,1,0:T(8,128)}) %reduce-scatter.2.cloned.1.call-update) | async-done | bytes 262160 | tf_op jit(solution)/shard_map/reduce_scatter | solution.py:85
  71.1 1.0 %constant_dynamic-slice_fusion = (f32[8,16,256]{2,1,0:T(8,128)S(1)}, f32[8,16,256]{2,1,0:T(8,128)S(1)}) fusion(f32[16,16,256]{2,1,0:T(8,128)} %reduce-scatter.2.cloned.1.call-done, s32[]{:T(128)S(6)} %select_n.220, s32[]{:T(128)S(6)} %select_n.221), kind=kLoop, calls=%fused_computation.68 | loop fusion | bytes 524296 | tf_op jit(solution)/shard_map/dynamic_slice | solution.py:88
  72.0 1.8 %collective-permute-start.6 = (f32[8,16,256]{2,1,0:T(8,128)S(1)}, f32[8,16,256]{2,1,0:T(8,128)S(1)}, u32[]{:S(2)}, u32[]{:S(2)}) collective-permute-start(f32[8,16,256]{2,1,0:T(8,128)S(1)} %get-tuple-element.12), channel_id=1, source_target_pairs={{0,2},{2,0},{4,6},{6,4},{8,10},{10,8},{12,14},{14,12},{16,18},{18,... | collective-permute-start | bytes 393224 | tf_op jit(solution)/shard_map/ppermute | solution.py:22
  73.8 4.0 %collective-permute-done.6 = f32[8,16,256]{2,1,0:T(8,128)S(1)} collective-permute-done((f32[8,16,256]{2,1,0:T(8,128)S(1)}, f32[8,16,256]{2,1,0:T(8,128)S(1)}, u32[]{:S(2)}, u32[]{:S(2)}) %collective-permute-start.6) | collective-permute-done | bytes 131104 | tf_op jit(solution)/shard_map/ppermute | solution.py:22
  77.8 0.7 maximum_select_fusion
  (51 shorter events, 3.9 us)
Async XLA Ops:
  6.5 64.5 %reduce-scatter.2.cloned.1.call-start = ((), (), s32[]{:S(2)}) async-start(), calls=%async_computation.1 | async-start | bytes 786432 | tf_op jit(solution)/shard_map/reduce_scatter | solution.py:85
  15.4 6.7 %copy-start.1 = (s32[1,1,16,128]{3,2,1,0:T(8,128)S(1)}, s32[1,1,16,128]{3,2,1,0:T(8,128)}, u32[]{:S(2)}) copy-start(s32[1,1,16,128]{3,2,1,0:T(8,128)} %param.8) | copy-start | bytes 24580
  15.4 6.7 %copy-start.2 = (bf16[1,1,16,128]{3,2,1,0:T(8,128)(2,1)S(1)}, bf16[1,1,16,128]{3,2,1,0:T(8,128)(2,1)}, u32[]{:S(2)}) copy-start(bf16[1,1,16,128]{3,2,1,0:T(8,128)(2,1)} %param.7) | copy-start | bytes 12292
  16.9 23.8 %copy-start = (s32[1,16,8]{1,2,0:T(8,128)S(1)}, s32[1,16,8]{1,2,0:T(8,128)}, u32[]{:S(2)}) copy-start(s32[1,16,8]{1,2,0:T(8,128)} %param.10) | copy-start | bytes 1540
  16.9 23.8 %copy-start.3 = (s32[6]{0:T(128)S(1)}, s32[6]{0:T(128)}, u32[]{:S(2)}) copy-start(s32[6]{0:T(128)} %constant.172) | copy-start | bytes 76
  26.9 23.4 %collective-permute-start.5 = (bf16[2,32,128]{2,1,0:T(8,128)(2,1)S(1)}, bf16[2,32,128]{2,1,0:T(8,128)(2,1)S(1)}, u32[]{:S(2)}, u32[]{:S(2)}) collective-permute-start(bf16[2,32,128]{2,1,0:T(8,128)(2,1)S(1)} %gather_fusion.6), channel_id=1, source_target_pairs={{0,24},{2,26},{4,28},{6,30},{8,0},{10,2},{12,4},{14,6},{16,8},{18,... | collective-permute-start | bytes 49160 | tf_op jit(solution)/shard_map/ppermute | solution.py:16
  32.4 17.8 %collective-permute-start.4 = (bf16[2,32,128]{2,1,0:T(8,128)(2,1)S(1)}, bf16[2,32,128]{2,1,0:T(8,128)(2,1)S(1)}, u32[]{:S(2)}, u32[]{:S(2)}) collective-permute-start(bf16[2,32,128]{2,1,0:T(8,128)(2,1)S(1)} %gather_fusion.5), channel_id=1, source_target_pairs={{0,8},{2,10},{4,12},{6,14},{8,16},{10,18},{12,20},{14,22},{16,24},... | collective-permute-start | bytes 49160 | tf_op jit(solution)/shard_map/ppermute | solution.py:16
  33.1 17.2 %collective-permute-start.3 = (bf16[2,32,128]{2,1,0:T(8,128)(2,1)S(1)}, bf16[2,32,128]{2,1,0:T(8,128)(2,1)S(1)}, u32[]{:S(2)}, u32[]{:S(2)}) collective-permute-start(bf16[2,32,128]{2,1,0:T(8,128)(2,1)S(1)} %gather_fusion.4), channel_id=1, source_target_pairs={{0,28},{2,30},{4,0},{6,2},{8,4},{10,6},{12,8},{14,10},{16,12},{18,... | collective-permute-start | bytes 49160 | tf_op jit(solution)/shard_map/ppermute | solution.py:16
  38.4 11.8 %collective-permute-start.2 = (bf16[2,32,128]{2,1,0:T(8,128)(2,1)S(1)}, bf16[2,32,128]{2,1,0:T(8,128)(2,1)S(1)}, u32[]{:S(2)}, u32[]{:S(2)}) collective-permute-start(bf16[2,32,128]{2,1,0:T(8,128)(2,1)S(1)} %gather_fusion.3), channel_id=1, source_target_pairs={{0,4},{2,6},{4,8},{6,10},{8,12},{10,14},{12,16},{14,18},{16,20},{1... | collective-permute-start | bytes 49160 | tf_op jit(solution)/shard_map/ppermute | solution.py:16
  39.1 7.4 %collective-permute-start = (bf16[2,32,128]{2,1,0:T(8,128)(2,1)S(1)}, bf16[2,32,128]{2,1,0:T(8,128)(2,1)S(1)}, u32[]{:S(2)}, u32[]{:S(2)}) collective-permute-start(bf16[2,32,128]{2,1,0:T(8,128)(2,1)S(1)} %gather_fusion.1), channel_id=1, source_target_pairs={{0,2},{2,4},{4,6},{6,8},{8,10},{10,12},{12,14},{14,16},{16,18},{18... | collective-permute-start | bytes 49160 | tf_op jit(solution)/shard_map/ppermute | solution.py:16
  46.5 3.7 %collective-permute-start.1 = (bf16[2,32,128]{2,1,0:T(8,128)(2,1)S(1)}, bf16[2,32,128]{2,1,0:T(8,128)(2,1)S(1)}, u32[]{:S(2)}, u32[]{:S(2)}) collective-permute-start(bf16[2,32,128]{2,1,0:T(8,128)(2,1)S(1)} %gather_fusion.2), channel_id=1, source_target_pairs={{0,30},{2,0},{4,2},{6,4},{8,6},{10,8},{12,10},{14,12},{16,14},{18,... | collective-permute-start | bytes 49160 | tf_op jit(solution)/shard_map/ppermute | solution.py:16
  72.0 5.7 %collective-permute-start.6 = (f32[8,16,256]{2,1,0:T(8,128)S(1)}, f32[8,16,256]{2,1,0:T(8,128)S(1)}, u32[]{:S(2)}, u32[]{:S(2)}) collective-permute-start(f32[8,16,256]{2,1,0:T(8,128)S(1)} %get-tuple-element.12), channel_id=1, source_target_pairs={{0,2},{2,0},{4,6},{6,4},{8,10},{10,8},{12,14},{14,12},{16,18},{18,... | collective-permute-start | bytes 393224 | tf_op jit(solution)/shard_map/ppermute | solution.py:22
Sparse Core Ops, SparseCore 0:
  61.7 9.3 reduce-scatter.1
where the time goes:
time: 85.7 us; the launch traced here: 85.4 us
  local copies, waits for them, and re-layouts  22.3 us (26%)
  waiting for transfers between devices  18.2 us (21%)
  starting transfers between devices  15.2 us (18%)
  between operations  13.6 us (16%)
  matrix products  7.5 us (9%)
  blocking collectives  6.03 us (7%)
  other arithmetic  2.44 us (3%)
    ppermute x6, starting transfers between devices, passed_along(): return lax.ppermute(value, axis, pairs)  13.5 us
    reduce_scatter x1, waiting for transfers between devices, per_device(): summed = lax.psum_scatter(coarse, 'sub', scatter_dimension=1, tiled=True)  9.48 us
    unnamed x14, local copies, waits for them, and re-layouts  7.77 us
    dot_general x1, matrix products, per_device(): jnp.einsum('bkgj,bkhj->bgkh', left_part, partner, preferred_element_type=...  5.81 us
    ppermute x6, waiting for transfers between devices, passed_along(): return lax.ppermute(value, axis, pairs)  4.71 us
    ppermute x1, waiting for transfers between devices, partner_2(): return lax.ppermute(value, axis, pairs)  3.98 us
    gather x6, local copies, waits for them, and re-layouts, per_device(): payload = smoothed[chosen]  3.35 us
    dynamic_slice x2, local copies, waits for them, and re-layouts, per_device(): lax.dynamic_slice_in_dim(diag_tile, sub_index * fine_rows, fine_rows, 2)  3.31 us
  transfers between devices with their start and end apart: 8, of which 4 were waited for; matrix products, arithmetic and copies ran while one was open for 4% of the time, Pallas kernels for 0%

commit v1 on v0

v1 whole, which is shorter than its diff:
```python
import functools

import jax
import jax.numpy as jnp
from jax import lax
from jax.experimental import pallas as pl
from jax.experimental.pallas import tpu as pltpu
from jax.sharding import PartitionSpec as P

AGGS = 32
OMEGA = 0.6666667
OFFSETS = (1, -1, 2, -2, 4, -4)
GROUP = 4
MESH = pl.DeviceIdType.MESH
NT = (((1,), (1,)), ((), ()))
NN = (((1,), (0,)), ((), ()))


def kernel(
    domains,
    null_ref,
    ids_ref,
    send_ref,
    recv_ref,
    c_hbm,
    out_ref,
    c_vmem,
    null_full,
    null_other,
    ids_full,
    sm_ref,
    pro_local,
    pro_remote,
    send_buf,
    left_ref,
    keep,
    xs_send,
    xs_recv,
    dom_send,
    dom_recv,
    table,
    load_sem,
    pair_sems,
    sm_sems,
    far_send_sems,
    far_recv_sems,
    xs_send_sems,
    xs_recv_sems,
    dom_send_sems,
    dom_recv_sems,
):
    blocks, neigh, rows, cols = c_hbm.shape
    half = blocks // 2
    groups = blocks // GROUP
    near = neigh // 2
    slots = send_ref.shape[1]
    me = lax.axis_index("dom")
    sub = lax.axis_index("sub")
    other = 1 - sub
    parity = lax.rem(me, 2)
    mate = me + 1 - 2 * parity
    first = half * (1 - parity)
    own_lanes = pl.ds(pl.multiple_of(sub * rows, rows), rows)
    other_lanes = pl.ds(pl.multiple_of(other * rows, rows), rows)
    is_low = sub == 0

    def group_start(group):
        return lax.rem(group * GROUP + first, blocks)

    diag_load = pltpu.make_async_copy(c_hbm.at[:, 0], c_vmem.at[:, 0], load_sem.at[groups])
    diag_load.start()

    def tile_load(group):
        span = pl.ds(group_start(group), GROUP)
        rest = pl.ds(1, neigh - 1)
        return pltpu.make_async_copy(
            c_hbm.at[span, rest], c_vmem.at[span, rest], load_sem.at[group]
        )

    for group in range(groups):
        tile_load(group).start()

    barrier = pltpu.get_barrier_semaphore()
    targets = [lax.rem(me + offset + domains, domains) for offset in OFFSETS]
    pl.semaphore_signal(barrier, inc=1, device_id=(me, other), device_id_type=MESH)
    for target in targets:
        for core in range(2):
            pl.semaphore_signal(barrier, inc=1, device_id=(target, core), device_id_type=MESH)

    null_full[:, own_lanes] = null_ref[...].astype(jnp.float32)
    ids_full[:, own_lanes] = ids_ref[...]

    def clear(place, carry):
        table[place] = 0
        return carry

    lax.fori_loop(0, domains * slots, clear, 0)
    for position, offset in enumerate(OFFSETS):
        source = lax.rem(me - offset + domains, domains)
        for slot in range(slots):
            table[source * slots + slot] = position * slots + slot

    pl.semaphore_wait(barrier, 1 + 2 * len(OFFSETS))

    null_copy = pltpu.make_async_remote_copy(
        null_ref, null_other, pair_sems.at[0], pair_sems.at[1], (me, other), MESH
    )
    ids_copy = pltpu.make_async_remote_copy(
        ids_ref, ids_full.at[:, own_lanes], pair_sems.at[2], pair_sems.at[3], (me, other), MESH
    )
    null_copy.start()
    ids_copy.start()
    diag_load.wait()
    null_copy.wait_recv()
    ids_copy.wait_recv()
    null_full[:, other_lanes] = null_other[...].astype(jnp.float32)

    labels = lax.broadcasted_iota(jnp.int32, (AGGS, cols), 0)
    on_diag = lax.broadcasted_iota(jnp.int32, (rows, rows), 0) == lax.broadcasted_iota(
        jnp.int32, (rows, rows), 1
    )

    def smooth_group(group, carry):
        for step in range(GROUP):
            block = group * GROUP + step
            values = null_full[pl.ds(block, 1), :]
            aggregate = ids_full[pl.ds(block, 1), :]
            scattered = jnp.where(aggregate == labels, values, 0.0)
            norm = jnp.sum(scattered * scattered, axis=1, keepdims=True)
            tentative = (scattered / jnp.sqrt(norm)).astype(jnp.bfloat16)
            wide = tentative.astype(jnp.float32)
            own = jnp.where(is_low, wide[:, :rows], wide[:, rows:])
            square = c_vmem[block, 0, :, own_lanes].astype(jnp.float32)
            diag = jnp.sum(jnp.where(on_diag, square, 0.0), axis=0, keepdims=True)
            smoothing = lax.dot_general(
                tentative, c_vmem[block, 0], NT, preferred_element_type=jnp.float32
            )
            smoothed = (own - smoothing * (OMEGA / diag)).astype(jnp.bfloat16)
            sm_ref[block] = smoothed
            pro_local[block, :, own_lanes] = smoothed
        return carry

    lax.fori_loop(0, groups, smooth_group, 0)

    sm_copy = pltpu.make_async_remote_copy(
        sm_ref, pro_local.at[:, :, own_lanes], sm_sems.at[0], sm_sems.at[1], (me, other), MESH
    )
    sm_copy.start()
    far_copies = []
    for position, target in enumerate(targets):
        for slot in range(slots):
            chosen = jnp.clip(send_ref[target, slot], 0, blocks - 1)
            send_buf[position, slot] = sm_ref[chosen]
        for core in range(2):
            copy = pltpu.make_async_remote_copy(
                send_buf.at[position],
                pro_remote.at[pl.ds(position * slots, slots), :, own_lanes],
                far_send_sems.at[position, core],
                far_recv_sems.at[position, sub],
                (target, core),
                MESH,
            )
            copy.start()
            far_copies.append(copy)

    def left_group(group, carry):
        tile_load(group).wait()
        for step in range(GROUP):
            block = group_start(group) + step
            smoothed = sm_ref[block]
            for tile in range(neigh):
                left = lax.dot_general(
                    smoothed, c_vmem[block, tile], NN, preferred_element_type=jnp.float32
                )
                left_ref[block, tile * AGGS : (tile + 1) * AGGS, :] = left.astype(jnp.bfloat16)
        return carry

    lax.fori_loop(0, groups, left_group, 0)

    sm_copy.wait_recv()
    for position, target in enumerate(targets):
        for core in range(2):
            pltpu.make_async_remote_copy(
                send_buf.at[position],
                pro_remote.at[
                    pl.ds(position * slots, slots), :, pl.ds(core * rows, rows)
                ],
                far_send_sems.at[position, core],
                far_recv_sems.at[position, core],
                (target, core),
                MESH,
            ).wait_recv()

    lane_tile = lax.broadcasted_iota(jnp.int32, (AGGS, near * AGGS), 1) // AGGS

    def tiles_of(left, partners):
        full = lax.dot_general(
            left, jnp.concatenate(partners, axis=0), NT, preferred_element_type=jnp.float32
        )
        picked = full[:AGGS]
        for tile in range(1, near):
            picked = jnp.where(lane_tile == tile, full[tile * AGGS : (tile + 1) * AGGS], picked)
        return picked

    cut = AGGS // 2

    def xs_copy(group):
        span = pl.ds(group * GROUP, GROUP)
        return pltpu.make_async_remote_copy(
            xs_send.at[span],
            xs_recv.at[span],
            xs_send_sems.at[group],
            xs_recv_sems.at[group],
            (me, other),
            MESH,
        )

    def dom_copy(group):
        span = pl.ds(group * GROUP, GROUP)
        return pltpu.make_async_remote_copy(
            dom_send.at[span],
            dom_recv.at[span],
            dom_send_sems.at[group],
            dom_recv_sems.at[group],
            (mate, sub),
            MESH,
        )

    def coarse_group(group):
        for step in range(GROUP):
            block = group_start(group) + step
            place = group * GROUP + step
            local = [pro_local[block]] + [
                pro_local[recv_ref[block, tile]] for tile in range(1, near)
            ]
            remote = [
                pro_remote[table[jnp.maximum(recv_ref[block, tile] - blocks, 0)]]
                for tile in range(near, neigh)
            ]
            width = near * AGGS
            for at, part in (
                (0, tiles_of(left_ref[block, :width, :], local)),
                (width, tiles_of(left_ref[block, width:, :], remote)),
            ):
                low, high = part[:cut], part[cut:]
                keep[place, :, at : at + width] = jnp.where(is_low, low, high)
                xs_send[place, :, at : at + width] = jnp.where(is_low, high, low).astype(
                    jnp.bfloat16
                )
        xs_copy(group).start()

    def total_of(group):
        xs_copy(group).wait_recv()
        span = pl.ds(group * GROUP, GROUP)
        return keep[span] + xs_recv[span].astype(jnp.float32)

    given = groups // 2

    def given_step(group, carry):
        coarse_group(group)
        return carry

    def kept_step(group, carry):
        coarse_group(group)
        done = group - given
        dom_send[pl.ds(done * GROUP, GROUP)] = total_of(done).astype(jnp.bfloat16)
        dom_copy(done).start()
        return carry

    lax.fori_loop(0, given, given_step, 0)
    lax.fori_loop(given, groups, kept_step, 0)

    def finish_kept(group, carry):
        place = pl.multiple_of(half * parity + (group - given) * GROUP, GROUP)
        out_ref[pl.ds(place, GROUP)] = total_of(group)
        return carry

    lax.fori_loop(given, groups, finish_kept, 0)

    def finish_given(group, carry):
        dom_copy(group).wait_recv()
        place = pl.multiple_of(first + group * GROUP, GROUP)
        out_ref[pl.ds(place, GROUP)] = dom_recv[pl.ds(group * GROUP, GROUP)].astype(jnp.float32)
        return carry

    lax.fori_loop(0, given, finish_given, 0)

    null_copy.wait_send()
    ids_copy.wait_send()
    sm_copy.wait_send()
    for copy in far_copies:
        copy.wait_send()
    for group in range(groups):
        xs_copy(group).wait_send()
    for group in range(given):
        dom_copy(group).wait_send()


def per_device(coupling, null_vector, aggregate_ids, send_list, recv_list):
    tiles = coupling[0, 0]
    blocks, neigh, rows, cols = tiles.shape
    domains = lax.axis_size("dom")
    slots = send_list.shape[2]
    half = blocks // 2
    groups = blocks // GROUP
    far = len(OFFSETS)
    bf16, f32, i32 = jnp.bfloat16, jnp.float32, jnp.int32
    vmem = pl.BlockSpec(memory_space=pltpu.VMEM)
    smem = pl.BlockSpec(memory_space=pltpu.SMEM)
    dma = pltpu.SemaphoreType.DMA
    return pl.pallas_call(
        functools.partial(kernel, domains),
        out_shape=jax.ShapeDtypeStruct((blocks, AGGS // 2, neigh * AGGS), f32),
        in_specs=[vmem, vmem, smem, smem, pl.BlockSpec(memory_space=pl.ANY)],
        out_specs=vmem,
        scratch_shapes=[
            pltpu.VMEM((blocks, neigh, rows, cols), bf16),
            pltpu.VMEM((blocks, cols), f32),
            pltpu.VMEM((blocks, rows), bf16),
            pltpu.VMEM((blocks, cols), i32),
            pltpu.VMEM((blocks, AGGS, rows), bf16),
            pltpu.VMEM((blocks, AGGS, cols), bf16),
            pltpu.VMEM((far * slots, AGGS, cols), bf16),
            pltpu.VMEM((far, slots, AGGS, rows), bf16),
            pltpu.VMEM((blocks, neigh * AGGS, cols), bf16),
            pltpu.VMEM((blocks, AGGS // 2, neigh * AGGS), f32),
            pltpu.VMEM((blocks, AGGS // 2, neigh * AGGS), bf16),
            pltpu.VMEM((blocks, AGGS // 2, neigh * AGGS), bf16),
            pltpu.VMEM((half, AGGS // 2, neigh * AGGS), bf16),
            pltpu.VMEM((half, AGGS // 2, neigh * AGGS), bf16),
            pltpu.SMEM((domains * slots,), i32),
            dma((groups + 1,)),
            dma((4,)),
            dma((2,)),
            dma((far, 2)),
            dma((far, 2)),
            dma((groups,)),
            dma((groups,)),
            dma((groups // 2,)),
            dma((groups // 2,)),
        ],
        compiler_params=pltpu.CompilerParams(
            collective_id=0, has_side_effects=True, vmem_limit_bytes=48 * 1024 * 1024
        ),
    )(null_vector[0, 0], aggregate_ids[0, 0], send_list[0], recv_list[0], tiles)


def solution(mesh):
    in_specs = (
        P("dom", "sub", None, None, None, None),
        P("dom", "sub", None, None),
        P("dom", "sub", None, None),
        P("dom", None, None),
        P("dom", None, None),
    )
    out_specs = P("dom", "sub", None)
    return jax.shard_map(
        per_device, mesh=mesh, in_specs=in_specs, out_specs=out_specs, check_vma=False
    )
```

time: 85.7 us -> 22.1 us (0.26)
  local copies, waits for them, and re-layouts: 22.3 us -> 3.6 us
  Pallas kernels: 0 us -> 18.3 us
  waiting for transfers between devices: 18.2 us -> 0 us
  starting transfers between devices: 15.2 us -> 0 us
  between operations: 13.6 us -> 0.01 us
  matrix products: 7.5 us -> 0 us
  blocking collectives: 6.03 us -> 0 us
  other arithmetic: 2.44 us -> 0 us
    pallas_call x0 -> x1, Pallas kernels: none -> 18.3 us  [per_device(): pl.pallas_call(functools.partial(kernel, domains), out_shape=jax.ShapeDty...]
    ppermute x7 -> x0, starting transfers between devices: 15.2 us -> none  [the longest x6 13.5 us: passed_along(): return lax.ppermute(value, axis, pairs)]
    reduce_scatter x1 -> x0, waiting for transfers between devices: 9.48 us -> none  [per_device(): summed = lax.psum_scatter(coarse, 'sub', scatter_dimension=1, tiled=True)]
    ppermute x7 -> x0, waiting for transfers between devices: 8.69 us -> none  [the longest x6 4.71 us: passed_along(): return lax.ppermute(value, axis, pairs)]
    dot_general x2 -> x0, matrix products: 7.5 us -> none  [the longest x1 5.81 us: per_device(): jnp.einsum('bkgj,bkhj->bgkh', left_part, partner, preferred_element_type=...]
    gather x8 -> x0, local copies, waits for them, and re-layouts: 7.35 us -> none  [the longest x6 3.35 us: per_device(): payload = smoothed[chosen]]
    all_gather x3 -> x0, blocking collectives: 6.03 us -> none  [the longest x1 2.09 us: per_device(): lax.all_gather(scattered, 'sub', axis=2, tiled=True).astype(jnp.float32)]
    unnamed x14 -> x5, local copies, waits for them, and re-layouts: 7.77 us -> 2.09 us
  transfers between devices with their start and end apart: 8 -> 0, of which waited for: 4 -> 0; matrix products, arithmetic and copies ran while one was open for 4% -> 0% of each run, Pallas kernels for 0% -> 0%
where the time goes in v1:
time: 22.1 us; the launch traced here: 21.9 us
  Pallas kernels  18.3 us (83%)
  local copies, waits for them, and re-layouts  3.6 us (16%)
    pallas_call x1, Pallas kernels, per_device(): pl.pallas_call(functools.partial(kernel, domains), out_shape=jax.ShapeDty...  18.3 us
    unnamed x5, local copies, waits for them, and re-layouts  2.09 us
    squeeze x1, local copies, waits for them, and re-layouts, per_device(): recv_list[0]  0.76 us
    squeeze x1, local copies, waits for them, and re-layouts, per_device(): send_list[0]  0.75 us

profile of v1, /device:TPU:0, one launch (start us, length us, event | category | flops | bytes accessed | tf_op | source)
XLA Modules:
  0.0 21.9 jit_solution(8366187088773262610)
XLA Ops:
  0.0 0.8 %copy.6.send_ref = s32[16,2]{1,0:T(8,128)S(1)} copy(s32[16,2]{0,1:T(2,128)} %bitcast.9) | data formatting | bytes 256 | tf_op jit(solution)/shard_map/squeeze | solution.py:345
  0.8 0.8 %copy.7.recv_ref = s32[16,8]{1,0:T(8,128)S(1)} copy(s32[16,8]{0,1:T(8,128)} %bitcast.8) | data formatting | bytes 1024 | tf_op jit(solution)/shard_map/squeeze | solution.py:345
  1.5 0.0 copy-start
  1.5 0.7 %copy-done = s32[1,1,16,128]{3,2,1,0:T(8,128)S(1)} copy-done((s32[1,1,16,128]{3,2,1,0:T(8,128)S(1)}, s32[1,1,16,128]{3,2,1,0:T(8,128)}, u32[]{:S(2)}) %copy-start) | copy-done | bytes 8216
  2.2 0.0 copy-start.1
  2.2 0.7 %copy-done.1 = bf16[1,1,16,128]{3,2,1,0:T(8,128)(2,1)S(1)} copy-done((bf16[1,1,16,128]{3,2,1,0:T(8,128)(2,1)S(1)}, bf16[1,1,16,128]{3,2,1,0:T(8,128)(2,1)}, u32[]{:S(2)}) %copy-start.1) | copy-done | bytes 4120
  2.9 18.3 %shard_map.55 = f32[16,16,256]{2,1,0:T(8,128)S(1)} custom-call(bf16[16,128]{1,0:T(8,128)(2,1)S(1)} %bitcast.6, s32[16,128]{1,0:T(8,128)S(1)} %bitcast.5, s32[16,2]{1,0:T(8,128)S(1)} %copy.6.send_ref, s32[16,8]{1,0:T(8,128)S(1)} %copy.7.recv_ref, bf16[16,8,128,256]{3,2,1,0:T(8,128)(2,1)} %bitcast.7), custom_call_target="tpu_custom_call" | custom-call | tf_op jit(solution)/shard_map/pallas_call | solution.py:311
  21.2 0.7 %copy.9 = f32[16,16,256]{2,1,0:T(8,128)} copy(f32[16,16,256]{2,1,0:T(8,128)S(1)} %shard_map.55) | data formatting | bytes 524288
Async XLA Ops:
  1.5 0.7 %copy-start = (s32[1,1,16,128]{3,2,1,0:T(8,128)S(1)}, s32[1,1,16,128]{3,2,1,0:T(8,128)}, u32[]{:S(2)}) copy-start(s32[1,1,16,128]{3,2,1,0:T(8,128)} %param.7) | copy-start | bytes 24580
  2.2 0.7 %copy-start.1 = (bf16[1,1,16,128]{3,2,1,0:T(8,128)(2,1)S(1)}, bf16[1,1,16,128]{3,2,1,0:T(8,128)(2,1)}, u32[]{:S(2)}) copy-start(bf16[1,1,16,128]{3,2,1,0:T(8,128)(2,1)} %param.6) | copy-start | bytes 12292

commit v2 on v1

--- a/solution.py
+++ b/solution.py
@@ -18,12 +18,16 @@
 
 def kernel(
     domains,
+    null_hbm,
+    ids_hbm,
+    send_hbm,
+    recv_hbm,
+    c_hbm,
+    out_ref,
     null_ref,
     ids_ref,
     send_ref,
     recv_ref,
-    c_hbm,
-    out_ref,
     c_vmem,
     null_full,
     null_other,
@@ -40,6 +44,7 @@
     dom_recv,
     table,
     load_sem,
+    small_sems,
     pair_sems,
     sm_sems,
     far_send_sems,
@@ -53,7 +58,7 @@
     half = blocks // 2
     groups = blocks // GROUP
     near = neigh // 2
-    slots = send_ref.shape[1]
+    slots = send_hbm.shape[0]
     me = lax.axis_index("dom")
     sub = lax.axis_index("sub")
     other = 1 - sub
@@ -67,6 +72,19 @@
     def group_start(group):
         return lax.rem(group * GROUP + first, blocks)
 
+    small_loads = [
+        pltpu.make_async_copy(source, target, small_sems.at[place])
+        for place, (source, target) in enumerate(
+            (
+                (null_hbm, null_ref),
+                (ids_hbm, ids_ref),
+                (send_hbm, send_ref),
+                (recv_hbm, recv_ref),
+            )
+        )
+    ]
+    for load in small_loads:
+        load.start()
     diag_load = pltpu.make_async_copy(c_hbm.at[:, 0], c_vmem.at[:, 0], load_sem.at[groups])
     diag_load.start()
 
@@ -87,6 +105,8 @@
         for core in range(2):
             pl.semaphore_signal(barrier, inc=1, device_id=(target, core), device_id_type=MESH)
 
+    small_loads[0].wait()
+    small_loads[1].wait()
     null_full[:, own_lanes] = null_ref[...].astype(jnp.float32)
     ids_full[:, own_lanes] = ids_ref[...]
 
@@ -146,10 +166,12 @@
         sm_ref, pro_local.at[:, :, own_lanes], sm_sems.at[0], sm_sems.at[1], (me, other), MESH
     )
     sm_copy.start()
+    small_loads[2].wait()
+    small_loads[3].wait()
     far_copies = []
     for position, target in enumerate(targets):
         for slot in range(slots):
-            chosen = jnp.clip(send_ref[target, slot], 0, blocks - 1)
+            chosen = jnp.clip(send_ref[slot, target], 0, blocks - 1)
             send_buf[position, slot] = sm_ref[chosen]
         for core in range(2):
             copy = pltpu.make_async_remote_copy(
@@ -178,6 +200,106 @@
     lax.fori_loop(0, groups, left_group, 0)
 
     sm_copy.wait_recv()
+
+    lane_tile = lax.broadcasted_iota(jnp.int32, (AGGS, near * AGGS), 1) // AGGS
+
+    def tiles_of(left, partners):
+        full = lax.dot_general(
+            left, jnp.concatenate(partners, axis=0), NT, preferred_element_type=jnp.float32
+        )
+        picked = full[:AGGS]
+        for tile in range(1, near):
+            picked = jnp.where(lane_tile == tile, full[tile * AGGS : (tile + 1) * AGGS], picked)
+        return picked
+
+    cut = AGGS // 2
+
+    def xs_copy(part, group):
+        span = pl.ds(group * GROUP, GROUP)
+        return pltpu.make_async_remote_copy(
+            xs_send.at[part, span],
+            xs_recv.at[part, span],
+            xs_send_sems.at[part, group],
+            xs_recv_sems.at[part, group],
+            (me, other),
+            MESH,
+        )
+
+    def dom_copy(part, group):
+        span = pl.ds(group * GROUP, GROUP)
+        return pltpu.make_async_remote_copy(
+            dom_send.at[part, span],
+            dom_recv.at[part, span],
+            dom_send_sems.at[part, group],
+            dom_recv_sems.at[part, group],
+            (mate, sub),
+            MESH,
+        )
+
+    width = near * AGGS
+
+    def coarse_group(part, group):
+        for step in range(GROUP):
+            block = group_start(group) + step
+            place = group * GROUP + step
+            if part == 0:
+                partners = [pro_local[block]] + [
+                    pro_local[recv_ref[tile, block]] for tile in range(1, near)
+                ]
+            else:
+                partners = [
+                    pro_remote[table[jnp.maximum(recv_ref[tile, block] - blocks, 0)]]
+                    for tile in range(near, neigh)
+                ]
+            tiles = tiles_of(left_ref[block, part * width : (part + 1) * width, :], partners)
+            low, high = tiles[:cut], tiles[cut:]
+            keep[part, place] = jnp.where(is_low, low, high)
+            xs_send[part, place] = jnp.where(is_low, high, low).astype(jnp.bfloat16)
+        xs_copy(part, group).start()
+
+    def total_of(part, group):
+        xs_copy(part, group).wait_recv()
+        span = pl.ds(group * GROUP, GROUP)
+        return keep[part, span] + xs_recv[part, span].astype(jnp.float32)
+
+    given = groups // 2
+
+    def column_part(part):
+        def given_step(group, carry):
+            coarse_group(part, group)
+            return carry
+
+        def kept_step(group, carry):
+            coarse_group(part, group)
+            done = group - given
+            dom_send[part, pl.ds(done * GROUP, GROUP)] = total_of(part, done).astype(jnp.bfloat16)
+            dom_copy(part, done).start()
+            return carry
+
+        lax.fori_loop(0, given, given_step, 0)
+        lax.fori_loop(given, groups, kept_step, 0)
+
+    def finish_part(part):
+        columns = slice(part * width, (part + 1) * width)
+
+        def finish_kept(group, carry):
+            place = half * parity + (group - given) * GROUP
+            out_ref[pl.ds(place, GROUP), :, columns] = total_of(part, group)
+            return carry
+
+        def finish_given(group, carry):
+            dom_copy(part, group).wait_recv()
+            place = first + group * GROUP
+            out_ref[pl.ds(place, GROUP), :, columns] = dom_recv[
+                part, pl.ds(group * GROUP, GROUP)
+            ].astype(jnp.float32)
+            return carry
+
+        lax.fori_loop(given, groups, finish_kept, 0)
+        return finish_given
+
+    column_part(0)
+
     for position, target in enumerate(targets):
         for core in range(2):
             pltpu.make_async_remote_copy(
@@ -190,110 +312,22 @@
                 (target, core),
                 MESH,
             ).wait_recv()
-
-    lane_tile = lax.broadcasted_iota(jnp.int32, (AGGS, near * AGGS), 1) // AGGS
-
-    def tiles_of(left, partners):
-        full = lax.dot_general(
-            left, jnp.concatenate(partners, axis=0), NT, preferred_element_type=jnp.float32
-        )
-        picked = full[:AGGS]
-        for tile in range(1, near):
-            picked = jnp.where(lane_tile == tile, full[tile * AGGS : (tile + 1) * AGGS], picked)
-        return picked
-
-    cut = AGGS // 2
-
-    def xs_copy(group):
-        span = pl.ds(group * GROUP, GROUP)
-        return pltpu.make_async_remote_copy(
-            xs_send.at[span],
-            xs_recv.at[span],
-            xs_send_sems.at[group],
-            xs_recv_sems.at[group],
-            (me, other),
-            MESH,
-        )
-
-    def dom_copy(group):
-        span = pl.ds(group * GROUP, GROUP)
-        return pltpu.make_async_remote_copy(
-            dom_send.at[span],
-            dom_recv.at[span],
-            dom_send_sems.at[group],
-            dom_recv_sems.at[group],
-            (mate, sub),
-            MESH,
-        )
-
-    def coarse_group(group):
-        for step in range(GROUP):
-            block = group_start(group) + step
-            place = group * GROUP + step
-            local = [pro_local[block]] + [
-                pro_local[recv_ref[block, tile]] for tile in range(1, near)
-            ]
-            remote = [
-                pro_remote[table[jnp.maximum(recv_ref[block, tile] - blocks, 0)]]
-                for tile in range(near, neigh)
-            ]
-            width = near * AGGS
-            for at, part in (
-                (0, tiles_of(left_ref[block, :width, :], local)),
-                (width, tiles_of(left_ref[block, width:, :], remote)),
-            ):
-                low, high = part[:cut], part[cut:]
-                keep[place, :, at : at + width] = jnp.where(is_low, low, high)
-                xs_send[place, :, at : at + width] = jnp.where(is_low, high, low).astype(
-                    jnp.bfloat16
-                )
-        xs_copy(group).start()
-
-    def total_of(group):
-        xs_copy(group).wait_recv()
-        span = pl.ds(group * GROUP, GROUP)
-        return keep[span] + xs_recv[span].astype(jnp.float32)
-
-    given = groups // 2
-
-    def given_step(group, carry):
-        coarse_group(group)
-        return carry
-
-    def kept_step(group, carry):
-        coarse_group(group)
-        done = group - given
-        dom_send[pl.ds(done * GROUP, GROUP)] = total_of(done).astype(jnp.bfloat16)
-        dom_copy(done).start()
-        return carry
-
-    lax.fori_loop(0, given, given_step, 0)
-    lax.fori_loop(given, groups, kept_step, 0)
-
-    def finish_kept(group, carry):
-        place = pl.multiple_of(half * parity + (group - given) * GROUP, GROUP)
-        out_ref[pl.ds(place, GROUP)] = total_of(group)
-        return carry
-
-    lax.fori_loop(given, groups, finish_kept, 0)
-
-    def finish_given(group, carry):
-        dom_copy(group).wait_recv()
-        place = pl.multiple_of(first + group * GROUP, GROUP)
-        out_ref[pl.ds(place, GROUP)] = dom_recv[pl.ds(group * GROUP, GROUP)].astype(jnp.float32)
-        return carry
-
-    lax.fori_loop(0, given, finish_given, 0)
+    column_part(1)
+    finish_local = finish_part(0)
+    lax.fori_loop(0, given, finish_local, 0)
+    finish_remote = finish_part(1)
+    lax.fori_loop(0, given, finish_remote, 0)
 
     null_copy.wait_send()
     ids_copy.wait_send()
     sm_copy.wait_send()
     for copy in far_copies:
         copy.wait_send()
-    for group in range(groups):
-        xs_copy(group).wait_send()
-    for group in range(given):
-        dom_copy(group).wait_send()
+    for part in range(2):
+        for group in range(groups):
+            xs_copy(part, group).wait_send()
+        for group in range(given):
+            dom_copy(part, group).wait_send()
 
 
 def per_device(coupling, null_vector, aggregate_ids, send_list, recv_list):
@@ -305,15 +339,18 @@
     groups = blocks // GROUP
     far = len(OFFSETS)
     bf16, f32, i32 = jnp.bfloat16, jnp.float32, jnp.int32
-    vmem = pl.BlockSpec(memory_space=pltpu.VMEM)
-    smem = pl.BlockSpec(memory_space=pltpu.SMEM)
+    hbm = pl.BlockSpec(memory_space=pltpu.HBM)
     dma = pltpu.SemaphoreType.DMA
     return pl.pallas_call(
         functools.partial(kernel, domains),
         out_shape=jax.ShapeDtypeStruct((blocks, AGGS // 2, neigh * AGGS), f32),
-        in_specs=[vmem, vmem, smem, smem, pl.BlockSpec(memory_space=pl.ANY)],
-        out_specs=vmem,
+        in_specs=[hbm] * 5,
+        out_specs=pl.BlockSpec(memory_space=pltpu.VMEM),
         scratch_shapes=[
+            pltpu.VMEM((blocks, rows), bf16),
+            pltpu.VMEM((blocks, rows), i32),
+            pltpu.SMEM((slots, domains), i32),
+            pltpu.SMEM((neigh, blocks), i32),
             pltpu.VMEM((blocks, neigh, rows, cols), bf16),
             pltpu.VMEM((blocks, cols), f32),
             pltpu.VMEM((blocks, rows), bf16),
@@ -323,26 +360,27 @@
             pltpu.VMEM((far * slots, AGGS, cols), bf16),
             pltpu.VMEM((far, slots, AGGS, rows), bf16),
             pltpu.VMEM((blocks, neigh * AGGS, cols), bf16),
-            pltpu.VMEM((blocks, AGGS // 2, neigh * AGGS), f32),
-            pltpu.VMEM((blocks, AGGS // 2, neigh * AGGS), bf16),
-            pltpu.VMEM((blocks, AGGS // 2, neigh * AGGS), bf16),
-            pltpu.VMEM((half, AGGS // 2, neigh * AGGS), bf16),
-            pltpu.VMEM((half, AGGS // 2, neigh * AGGS), bf16),
+            pltpu.VMEM((2, blocks, AGGS // 2, neigh // 2 * AGGS), f32),
+            pltpu.VMEM((2, blocks, AGGS // 2, neigh // 2 * AGGS), bf16),
+            pltpu.VMEM((2, blocks, AGGS // 2, neigh // 2 * AGGS), bf16),
+            pltpu.VMEM((2, half, AGGS // 2, neigh // 2 * AGGS), bf16),
+            pltpu.VMEM((2, half, AGGS // 2, neigh // 2 * AGGS), bf16),
             pltpu.SMEM((domains * slots,), i32),
             dma((groups + 1,)),
+            dma((4,)),
             dma((4,)),
             dma((2,)),
             dma((far, 2)),
             dma((far, 2)),
-            dma((groups,)),
-            dma((groups,)),
-            dma((groups // 2,)),
-            dma((groups // 2,)),
+            dma((2, groups)),
+            dma((2, groups)),
+            dma((2, groups // 2)),
+            dma((2, groups // 2)),
         ],
         compiler_params=pltpu.CompilerParams(
-            collective_id=0, has_side_effects=True, vmem_limit_bytes=48 * 1024 * 1024
+            collective_id=0, has_side_effects=True, vmem_limit_bytes=64 * 1024 * 1024
         ),
-    )(null_vector[0, 0], aggregate_ids[0, 0], send_list[0], recv_list[0], tiles)
+    )(null_vector[0, 0], aggregate_ids[0, 0], send_list[0].T, recv_list[0].T, tiles)
 
 
 def solution(mesh):

time: 22.1 us -> 19.2 us (0.87)
  local copies, waits for them, and re-layouts: 3.6 us -> 1.67 us
  Pallas kernels: 18.3 us -> 17.4 us
    squeeze x2 -> x0, local copies, waits for them, and re-layouts: 1.51 us -> none  [the longest x1 0.76 us: per_device(): recv_list[0]]
    pallas_call x1, Pallas kernels: 18.3 us -> 17.4 us  [per_device(): pl.pallas_call(functools.partial(kernel, domains), out_shape=jax.ShapeDty...]
    unnamed x5 -> x1, local copies, waits for them, and re-layouts: 2.09 us -> 1.67 us
where the time goes in v2:
time: 19.2 us; the launch traced here: 19.1 us
  Pallas kernels  17.4 us (91%)
  local copies, waits for them, and re-layouts  1.67 us (9%)
    pallas_call x1, Pallas kernels, per_device(): pl.pallas_call(functools.partial(kernel, domains), out_shape=jax.ShapeDty...  17.4 us
    unnamed x1, local copies, waits for them, and re-layouts  1.67 us

profile of v2, /device:TPU:0, one launch (start us, length us, event | category | flops | bytes accessed | tf_op | source)
XLA Modules:
  0.0 19.1 jit_solution(1691365407282612962)
XLA Ops:
  0.0 17.4 %shard_map.55 = f32[16,16,256]{2,1,0:T(8,128)} custom-call(bf16[16,128]{1,0:T(8,128)(2,1)} %bitcast.11, s32[16,128]{1,0:T(8,128)} %bitcast.10, s32[2,16]{1,0:T(2,128)} %bitcast.13, s32[8,16]{1,0:T(8,128)} %bitcast.12, bf16[16,8,128,256]{3,2,1,0:T(8,128)(2,1)} %bitcast.9), custom_call_target="tpu_custom_call" | custom-call | tf_op jit(solution)/shard_map/pallas_call | solution.py:344
  17.4 1.7 %copy.7 = f32[16,16,256]{2,1,0:T(8,128)} copy(f32[16,16,256]{2,1,0:T(8,128)} %shard_map.55) | data formatting | bytes 524288

commit v3 on v2

--- a/solution.py
+++ b/solution.py
@@ -299,6 +299,8 @@
         return finish_given
 
     column_part(0)
+    finish_local = finish_part(0)
+    lax.fori_loop(0, given, finish_local, 0)
 
     for position, target in enumerate(targets):
         for core in range(2):
@@ -313,8 +315,6 @@
                 MESH,
             ).wait_recv()
     column_part(1)
-    finish_local = finish_part(0)
-    lax.fori_loop(0, given, finish_local, 0)
     finish_remote = finish_part(1)
     lax.fori_loop(0, given, finish_remote, 0)
 

time: 19.2 us -> 22 us (1.15)
  Pallas kernels: 17.4 us -> 20.2 us
    pallas_call x1, Pallas kernels: 17.4 us -> 20.2 us  [per_device(): pl.pallas_call(functools.partial(kernel, domains), out_shape=jax.ShapeDty...]
where the time goes in v3:
time: 22 us; the launch traced here: 21.8 us
  Pallas kernels  20.2 us (92%)
  local copies, waits for them, and re-layouts  1.67 us (8%)
    pallas_call x1, Pallas kernels, per_device(): pl.pallas_call(functools.partial(kernel, domains), out_shape=jax.ShapeDty...  20.2 us
    unnamed x1, local copies, waits for them, and re-layouts  1.67 us

profile of v3, /device:TPU:0, one launch (start us, length us, event | category | flops | bytes accessed | tf_op | source)
XLA Modules:
  0.0 21.8 jit_solution(1952947874651275218)
XLA Ops:
  0.0 20.2 %shard_map.55 = f32[16,16,256]{2,1,0:T(8,128)} custom-call(bf16[16,128]{1,0:T(8,128)(2,1)} %bitcast.11, s32[16,128]{1,0:T(8,128)} %bitcast.10, s32[2,16]{1,0:T(2,128)} %bitcast.13, s32[8,16]{1,0:T(8,128)} %bitcast.12, bf16[16,8,128,256]{3,2,1,0:T(8,128)(2,1)} %bitcast.9), custom_call_target="tpu_custom_call" | custom-call | tf_op jit(solution)/shard_map/pallas_call | solution.py:344
  20.2 1.7 %copy.7 = f32[16,16,256]{2,1,0:T(8,128)} copy(f32[16,16,256]{2,1,0:T(8,128)} %shard_map.55) | data formatting | bytes 524288
